TPU v7x, 32 devices: a whole 2x2x4 slice. The times are simulated.
32 devices in a mesh: cam: 4 (over y, core), frame: 8 (over z, x).
Axes of the slice: x: 2, y: 2, z: 4, core: 2. Of those that a mesh axis runs over, the one named last changes fastest.
Arguments:
- tokens: bfloat16 [8, 8, 256, 1152], P('cam', 'frame'), may hold values from -6 to 6
- counts: int32 [8, 8], P('cam', 'frame'), may hold values from 1 to 4, as said below
- neighbours: int32 [8, 2], P('cam'), may hold values from 0 to 7, as said below
- side_keys: bfloat16 [2, 576], replicated, may hold values from -5 to 5
- cross_qkv: bfloat16 [1152, 1728], replicated, may hold values from -2 to 2
- cross_out: bfloat16 [576, 1152], replicated, may hold values from -0.25 to 0.25
- time_qkv: bfloat16 [1152, 1728], replicated, may hold values from -2 to 2
- time_out: bfloat16 [576, 1152], replicated, may hold values from -0.25 to 0.25
Outputs:
- block_output: bfloat16 [8, 8, 256, 1152], P('cam', 'frame')
Inputs may be any that keep to these rules, and one draw needn't show every extreme that they name: `counts`: in every camera some frame is full, with 4 rows. Row c holds camera c's cycle neighbours (c - 1) mod 8 and (c + 1) mod 8, in either order.
All inputs are finite; a program needn't handle non-finite values.
Results may differ from a plain program's by a relative error of at most 0.017.
The roundings to bfloat16 on the way count: a program that leaves them out, or rounds other values in their place, can miss the bound.
Values may be sent and summed in bfloat16 or wider, within the bound.
A program may use at most 128 MiB of HBM per device.

v0:
```python
import jax
import jax.numpy as jnp
from jax import lax
from jax.sharding import PartitionSpec as P

HEADS = 8


epsilon = 1e-06
row_tokens = 64


def passed_along(x, axis, by):
    peers = lax.axis_size(axis)
    return lax.ppermute(x, axis, [(i, (i + by) % peers) for i in range(peers)])


def normalize(values):
    values = values.astype(jnp.float32)
    mean = jnp.mean(values, axis=-1, keepdims=True)
    centred = values - mean
    variance = jnp.mean(centred * centred, axis=-1, keepdims=True)
    return (centred * lax.rsqrt(variance + epsilon)).astype(jnp.bfloat16)


def project(normed, weight):
    flat = normed.reshape(-1, normed.shape[-1])
    result = jnp.dot(flat, weight, preferred_element_type=jnp.float32)
    return result.reshape(normed.shape[:-1] + (weight.shape[1],))


def softmax_rows(scores, allowed):
    masked = jnp.where(allowed, scores, -1e30)
    highest = jnp.max(masked, axis=-1, keepdims=True)
    expo = jnp.exp(masked - highest)
    return (expo / jnp.sum(expo, axis=-1, keepdims=True)).astype(jnp.bfloat16)


def temporal_tail(projected, arrived, time_out):
    cams_here, frames, places, _ = projected.shape
    inner = time_out.shape[0]
    head_size = inner // HEADS
    query_heads = projected[..., :inner].reshape(cams_here, frames, places, HEADS, head_size)
    key_heads = projected[..., inner : 2 * inner].reshape(
        cams_here, frames, places, HEADS, head_size
    )
    value_heads = projected[..., 2 * inner :].reshape(cams_here, frames, places, HEADS, head_size)
    scores = jnp.einsum(
        "cfphd,cgphd->cphfg", query_heads, key_heads, preferred_element_type=jnp.float32
    ) * head_size ** (-0.5)
    allowed = (jnp.transpose(arrived, (0, 2, 1)) > 0.5)[:, :, None, None, :]
    allowed = allowed | jnp.eye(frames, dtype=jnp.bool_)[None, None, None]
    probs = softmax_rows(scores, allowed)
    attended = jnp.einsum(
        "cphfg,cgphd->cfphd", probs, value_heads, preferred_element_type=jnp.float32
    )
    attended = attended.astype(jnp.bfloat16).reshape(cams_here, frames, places, inner)
    returned = lax.all_to_all(attended, "frame", split_axis=1, concat_axis=2, tiled=True)
    return project(returned, time_out)


def shards(tokens, counts, neighbours, side_keys, cross_qkv, cross_out, time_qkv, time_out):
    cam_here, frames_here, token_count, width = tokens.shape
    inner = cross_out.shape[0]
    head_size = inner // HEADS
    position = lax.broadcasted_iota(jnp.int32, (cam_here, frames_here, token_count), 2)
    valid = (position < row_tokens * counts[:, :, None]).astype(jnp.bfloat16)
    projected = project(normalize(tokens), cross_qkv).astype(jnp.bfloat16)
    query = projected[..., :inner]
    keys = projected[..., inner : 2 * inner]
    values = projected[..., 2 * inner :]
    left_keys, left_values, left_valid = passed_along((keys[-1], values[-1], valid[-1]), "cam", 1)
    right_keys, right_values, right_valid = passed_along((keys[0], values[0], valid[0]), "cam", -1)
    lower_keys = jnp.concatenate([left_keys[None], keys[:-1]], axis=0)
    lower_values = jnp.concatenate([left_values[None], values[:-1]], axis=0)
    lower_valid = jnp.concatenate([left_valid[None], valid[:-1]], axis=0)
    upper_keys = jnp.concatenate([keys[1:], right_keys[None]], axis=0)
    upper_values = jnp.concatenate([values[1:], right_values[None]], axis=0)
    upper_valid = jnp.concatenate([valid[1:], right_valid[None]], axis=0)
    cameras = cam_here * lax.axis_size("cam")
    cam_ids = cam_here * lax.axis_index("cam") + jnp.arange(cam_here, dtype=jnp.int32)
    first_lower = neighbours[:, 0] == (cam_ids - 1) % cameras
    side_lower = jnp.where(first_lower[:, None], side_keys[0][None], side_keys[1][None]).astype(
        jnp.float32
    )
    side_upper = jnp.where(first_lower[:, None], side_keys[1][None], side_keys[0][None]).astype(
        jnp.float32
    )
    lower_keys = (lower_keys.astype(jnp.float32) + side_lower[:, None, None, :]).astype(
        jnp.bfloat16
    )
    upper_keys = (upper_keys.astype(jnp.float32) + side_upper[:, None, None, :]).astype(
        jnp.bfloat16
    )
    all_keys = jnp.concatenate([keys, lower_keys, upper_keys], axis=2)
    all_values = jnp.concatenate([values, lower_values, upper_values], axis=2)
    all_valid = jnp.concatenate([valid, lower_valid, upper_valid], axis=2)
    items = cam_here * frames_here
    query_heads = query.reshape(items, token_count, HEADS, head_size)
    key_heads = all_keys.reshape(items, 3 * token_count, HEADS, head_size)
    value_heads = all_values.reshape(items, 3 * token_count, HEADS, head_size)
    scores = jnp.einsum(
        "bqhd,bkhd->bhqk", query_heads, key_heads, preferred_element_type=jnp.float32
    ) * head_size ** (-0.5)
    allowed = (all_valid.reshape(items, 3 * token_count) > 0.5)[:, None, None, :]
    probs = softmax_rows(scores, allowed)
    attended = jnp.einsum("bhqk,bkhd->bqhd", probs, value_heads, preferred_element_type=jnp.float32)
    attended = attended.astype(jnp.bfloat16).reshape(cam_here, frames_here, token_count, inner)
    mixed = (project(attended, cross_out) + tokens.astype(jnp.float32)).astype(jnp.bfloat16)
    normed = normalize(mixed)
    time_proj = project(normed, time_qkv).astype(jnp.bfloat16)
    temporal = temporal_tail(
        lax.all_to_all(time_proj, "frame", split_axis=2, concat_axis=1, tiled=True),
        lax.all_to_all(valid, "frame", split_axis=2, concat_axis=1, tiled=True),
        time_out,
    )
    return (temporal + mixed.astype(jnp.float32)).astype(jnp.bfloat16)


def solution(mesh):
    return jax.shard_map(
        shards,
        mesh=mesh,
        in_specs=(
            P("cam", "frame", None, None),
            P("cam", "frame"),
            P("cam", None),
            P(),
            P(),
            P(),
            P(),
            P(),
        ),
        out_specs=P("cam", "frame", None, None),
        check_vma=False,
    )
```

profile of v0, /device:TPU:0, one launch (start us, length us, event | category | flops | bytes accessed | tf_op | source)
XLA Modules:
  0.0 143.0 jit_solution(3968319832591338489)
XLA Ops:
  0.0 1.6 %convert_reduce_fusion.1 = f32[2,256]{1,0:T(2,128)S(1)} fusion(bf16[2,1,256,1152]{3,2,1,0:T(8,128)(2,1)} %param.8), kind=kLoop, calls=%fused_computation.19 | loop fusion | flops 1179136 | bytes 1181696 | tf_op jit(solution)/shard_map/reduce_sum | solution.py:20
  1.7 1.7 %fusion.29 = f32[2,256]{1,0:T(2,128)S(1)} fusion(bf16[2,1,256,1152]{3,2,1,0:T(8,128)(2,1)} %param.8, f32[2,256]{1,0:T(2,128)S(1)} %broadcast_multiply_fusion.1), kind=kLoop, calls=%fused_computation.34 | loop fusion | flops 2358784 | bytes 1183744 | tf_op jit(solution)/shard_map/reduce_sum | solution.py:22
  3.4 4.8 %fusion.11 = bf16[2,256,1728]{1,2,0:T(8,128)(2,1)S(1)} fusion(bf16[1152,1728]{0,1:T(8,128)(2,1)} %param.12, bf16[2,1,256,1152]{3,2,1,0:T(8,128)(2,1)S(1)} %copy-done.1, f32[2,256]{1,0:T(2,128)S(1)} %add_rsqrt_fusion.1, f32[2,256]{1,0:T(2,128)S(1)} %broadcast_multiply_fusion.1), kind=kOutput, calls=%fused_computation.22 | convolution fusion | flops 2041675776 | bytes 6934528 | tf_op jit(solution)/shard_map/dot_general | solution.py:28
  8.2 1.3 slice_bitcast_fusion.5
  9.6 2.4 %collective-permute-start.1 = (bf16[1,256,576]{1,2,0:T(8,128)(2,1)}, bf16[1,256,576]{1,2,0:T(8,128)(2,1)}, u32[]{:S(2)}, u32[]{:S(2)}) collective-permute-start(bf16[1,256,576]{1,2,0:T(8,128)(2,1)} %get-tuple-element.14), channel_id=1, source_target_pairs={{0,24},{8,0},{16,8},{24,16},{1,25},{9,1},{17,9},{25,17},{2,26},{10... | collective-permute-start | bytes 884744 | tf_op jit(solution)/shard_map/ppermute | solution.py:15
  12.0 0.7 slice_bitcast_fusion.6
  12.7 1.7 %collective-permute-start.5 = (bf16[1,256,576]{1,2,0:T(8,128)(2,1)}, bf16[1,256,576]{1,2,0:T(8,128)(2,1)}, u32[]{:S(2)}, u32[]{:S(2)}) collective-permute-start(bf16[1,256,576]{1,2,0:T(8,128)(2,1)} %get-tuple-element.13), channel_id=1, source_target_pairs={{0,24},{8,0},{16,8},{24,16},{1,25},{9,1},{17,9},{25,17},{2,26},{10... | collective-permute-start | bytes 884744 | tf_op jit(solution)/shard_map/ppermute | solution.py:15
  14.5 0.6 slice_bitcast_fusion.3
  15.7 0.8 copy.70
  16.5 5.8 %all-to-all-start.1 = ((bf16[2,1,256]{0,1,2:T(2,128)(2,1)}), bf16[2,1,256]{0,1,2:T(2,128)(2,1)S(1)}, u32[]{:S(2)}, u32[]{:S(2)}) async-start(bf16[2,1,256]{0,1,2:T(2,128)(2,1)} %copy.70), calls=%async_computation.1 | async-start | bytes 262144 | tf_op jit(solution)/shard_map/all_to_all | solution.py:114
  22.3 1.1 fusion.66
  23.6 0.9 compare_reduce_fusion
  24.6 0.9 slice.72
  25.5 1.3 add_convert_fusion
  26.8 5.0 %collective-permute-done.4 = bf16[1,256,576]{1,2,0:T(8,128)(2,1)S(1)} collective-permute-done((bf16[1,256,576]{1,2,0:T(8,128)(2,1)}, bf16[1,256,576]{1,2,0:T(8,128)(2,1)S(1)}, u32[]{:S(2)}, u32[]{:S(2)}) %collective-permute-start.4) | collective-permute-done | bytes 294944 | tf_op jit(solution)/shard_map/ppermute | solution.py:15
  32.1 1.8 %fusion.32 = f32[2,8,256,768]{3,2,1,0:T(8,128)S(1)} fusion(bf16[2,256,8,72]{1,3,2,0:T(8,128)(2,1)S(1)} %bitcast.116, bf16[2,256,8,72]{1,3,2,0:T(8,128)(2,1)S(1)} %add_convert_fusion, bf16[2,256,8,72]{1,3,2,0:T(8,128)(2,1)S(1)} %add_convert_fusion.1, bf16[2,256,8,72]{1,3,2,0:T(8,128)(2,1)S(1)} %bitcast.115), kind=kOutput, calls=%fused_computation.41 | convolution fusion | flops 458293248 | bytes 14942208 | tf_op jit(solution)/shard_map/bqhd,bkhd->bhqk/dot_general | solution.py:102
  33.9 7.0 %fusion.67 = (f32[2,8,256]{2,1,0:T(8,128)S(1)}, f32[2,8,256,768]{3,2,1,0:T(8,128)}) fusion(f32[2,8,256,768]{3,2,1,0:T(8,128)S(1)} %fusion.32, pred[2,768]{1,0:T(4,128)(4,1)S(1)} %bitcast.123), kind=kOutput, calls=%fused_computation.103 | output fusion | flops 18875136 | bytes 25183744 | tf_op jit(solution)/shard_map/sub | solution.py:35
  41.0 1.2 maximum_maximum_fusion
  42.2 6.8 %fusion.41 = bf16[2,8,72,256]{3,2,1,0:T(8,128)(2,1)S(1)} fusion(bf16[2,768,8,72]{1,3,2,0:T(8,128)(2,1)S(1)} %bitcast.117, f32[2,8,256,768]{3,2,1,0:T(8,128)} %get-tuple-element.27, f32[2,8,256]{2,1,0:T(8,128)S(1)} %get-tuple-element.26), kind=kOutput, calls=%fused_computation.51 | convolution fusion | flops 459571200 | bytes 14958592 | tf_op jit(solution)/shard_map/bhqk,bkhd->bqhd/dot_general | solution.py:107
  49.0 1.4 convert_reduce_fusion
  51.4 2.8 %fusion.24 = bf16[2,1,256,1728]{2,3,0,1:T(8,128)(2,1)S(1)} fusion(bf16[1152,1728]{0,1:T(8,128)(2,1)S(1)} %copy-done.11, bf16[2,1,256,1152]{3,2,0,1:T(8,128)(2,1)S(1)} %get-tuple-element.29, f32[2,256]{1,0:T(2,128)S(1)} %add_rsqrt_fusion, f32[2,256]{1,0:T(2,128)S(1)} %broadcast_multiply_fusion), kind=kOutput, calls=%fused_computation.31 | convolution fusion | flops 2041675776 | bytes 6934528 | tf_op jit(solution)/shard_map/dot_general | solution.py:28
  54.2 3.6 %copy.68 = bf16[2,1,256,1728]{3,0,1,2:T(2,128)(2,1)} copy(bf16[2,1,256,1728]{2,3,0,1:T(8,128)(2,1)S(1)} %fusion.24) | data formatting | bytes 3538944 | tf_op jit(solution)/shard_map/convert_element_type | solution.py:111
  57.8 6.0 %all-to-all-start = ((bf16[2,1,256,1728]{3,0,1,2:T(2,128)(2,1)}), bf16[2,1,256,1728]{3,0,1,2:T(2,128)(2,1)S(1)}, u32[]{:S(2)}, u32[]{:S(2)}) async-start(bf16[2,1,256,1728]{3,0,1,2:T(2,128)(2,1)} %copy.68), calls=%async_computation | async-start | bytes 3670016 | tf_op jit(solution)/shard_map/all_to_all | solution.py:113
  64.3 40.8 %all-to-all-done = bf16[2,1,256,1728]{3,0,1,2:T(2,128)(2,1)S(1)} async-done(((bf16[2,1,256,1728]{3,0,1,2:T(2,128)(2,1)}), bf16[2,1,256,1728]{3,0,1,2:T(2,128)(2,1)S(1)}, u32[]{:S(2)}, u32[]{:S(2)}) %all-to-all-start) | async-done | bytes 1769504 | tf_op jit(solution)/shard_map/all_to_all | solution.py:113
  105.8 2.0 %reshape.336 = bf16[2,8,32,8,72]{4,3,2,1,0:T(8,128)(2,1)} reshape(bf16[2,8,32,576]{3,2,1,0:T(8,128)(2,1)S(1)} %get-tuple-element.8) | data formatting | bytes 1179648 | tf_op jit(solution)/shard_map/reshape | solution.py:44
  107.8 2.0 %reshape.335 = bf16[2,8,32,8,72]{4,3,2,1,0:T(8,128)(2,1)} reshape(bf16[2,8,32,576]{3,2,1,0:T(8,128)(2,1)S(1)} %get-tuple-element.9) | data formatting | bytes 1179648 | tf_op jit(solution)/shard_map/reshape | solution.py:43
  109.8 1.0 reshape.334
  110.9 5.1 %fusion.68 = (f32[2,32,8,8]{3,2,1,0:T(8,128)S(1)}, f32[2,32,8,8,8]{3,4,2,1,0:T(8,128)}) fusion(pred[2,32,8,8]{2,3,1,0:T(8,128)(4,1)S(1)} %broadcast_or_fusion, bf16[2,8,32,8,72]{4,3,2,1,0:T(8,128)(2,1)} %reshape.336, bf16[2,8,32,8,72]{4,3,2,1,0:T(8,128)(2,1)} %reshape.335), kind=kOutput, calls=%fused_computation.104 | convolution fusion | flops 4849671 | bytes 1331200 | tf_op jit(solution)/shard_map/sub | solution.py:35
  116.0 2.6 %fusion.38 = bf16[2,8,32,8,72]{4,1,3,2,0:T(8,128)(2,1)S(1)} fusion(f32[2,32,8,8,8]{3,4,2,1,0:T(8,128)} %get-tuple-element.31, bf16[2,8,32,8,72]{4,3,2,1,0:T(8,128)(2,1)S(1)} %reshape.334, f32[2,32,8,8]{3,2,1,0:T(8,128)S(1)} %get-tuple-element.30), kind=kOutput, calls=%fused_computation.48 | convolution fusion | flops 5079040 | bytes 1327104 | tf_op jit(solution)/shard_map/cphfg,cgphd->cfphd/dot_general | solution.py:54
  118.8 0.8 reshape.343
  119.6 21.1 %all_to_all.30 = bf16[2,8,32,576]{3,2,0,1:T(8,128)(2,1)S(1)} all-to-all(bf16[2,8,32,576]{3,2,0,1:T(8,128)(2,1)S(1)} %reshape.343), channel_id=1, replica_groups=mesh['cam'=4,'frame'=8] {'frame'}, dimensions={1} | all-to-all | bytes 1179648 | tf_op jit(solution)/shard_map/all_to_all | solution.py:58
  140.8 2.2 %fusion.23 = bf16[2,1,256,1152]{3,2,1,0:T(8,128)(2,1)} fusion(bf16[2,1,256,1152]{3,2,0,1:T(8,128)(2,1)S(1)} %copy-done.8, bf16[2,256,576]{2,1,0:T(8,128)(2,1)S(1)} %bitcast.120, bf16[576,1152]{1,0:T(8,128)(2,1)S(1)} %copy-done.12), kind=kOutput, calls=%fused_computation.30 | convolution fusion | flops 681246720 | bytes 4276224 | tf_op jit(solution)/shard_map/dot_general | solution.py:28
  (62 shorter events, 3.6 us)
Async XLA Ops:
  0.0 49.0 %copy-start = (bf16[576,1152]{1,0:T(8,128)(2,1)S(1)}, bf16[576,1152]{1,0:T(8,128)(2,1)}, u32[]{:S(2)}) copy-start(bf16[576,1152]{1,0:T(8,128)(2,1)} %param.13) | copy-start | bytes 3981316
  0.0 3.4 %copy-start.1 = (bf16[2,1,256,1152]{3,2,1,0:T(8,128)(2,1)S(1)}, bf16[2,1,256,1152]{3,2,1,0:T(8,128)(2,1)}, u32[]{:S(2)}) copy-start(bf16[2,1,256,1152]{3,2,1,0:T(8,128)(2,1)} %param.8) | copy-start | bytes 3538948
  8.2 6.2 %copy-start.13 = (s32[2,1]{0,1:T(1,128)S(1)}, s32[2,1]{0,1:T(1,128)}, u32[]{:S(2)}) copy-start(s32[2,1]{0,1:T(1,128)} %param.9) | copy-start | bytes 28
  9.6 13.8 %copy-start.10 = (bf16[2,576]{1,0:T(2,128)(2,1)S(1)}, bf16[2,576]{1,0:T(2,128)(2,1)}, u32[]{:S(2)}) copy-start(bf16[2,576]{1,0:T(2,128)(2,1)} %param.11) | copy-start | bytes 6916
  9.6 31.4 %collective-permute-start.1 = (bf16[1,256,576]{1,2,0:T(8,128)(2,1)}, bf16[1,256,576]{1,2,0:T(8,128)(2,1)}, u32[]{:S(2)}, u32[]{:S(2)}) collective-permute-start(bf16[1,256,576]{1,2,0:T(8,128)(2,1)} %get-tuple-element.14), channel_id=1, source_target_pairs={{0,24},{8,0},{16,8},{24,16},{1,25},{9,1},{17,9},{25,17},{2,26},{10... | collective-permute-start | bytes 884744 | tf_op jit(solution)/shard_map/ppermute | solution.py:15
  12.7 28.2 %collective-permute-start = (bf16[1,256,576]{1,2,0:T(8,128)(2,1)}, bf16[1,256,576]{1,2,0:T(8,128)(2,1)}, u32[]{:S(2)}, u32[]{:S(2)}) collective-permute-start(bf16[1,256,576]{1,2,0:T(8,128)(2,1)} %get-tuple-element.18), channel_id=1, source_target_pairs={{0,8},{8,16},{16,24},{24,0},{1,9},{9,17},{17,25},{25,1},{2,10},{10... | collective-permute-start | bytes 884744 | tf_op jit(solution)/shard_map/ppermute | solution.py:15
  12.7 12.8 %collective-permute-start.5 = (bf16[1,256,576]{1,2,0:T(8,128)(2,1)}, bf16[1,256,576]{1,2,0:T(8,128)(2,1)}, u32[]{:S(2)}, u32[]{:S(2)}) collective-permute-start(bf16[1,256,576]{1,2,0:T(8,128)(2,1)} %get-tuple-element.13), channel_id=1, source_target_pairs={{0,24},{8,0},{16,8},{24,16},{1,25},{9,1},{17,9},{25,17},{2,26},{10... | collective-permute-start | bytes 884744 | tf_op jit(solution)/shard_map/ppermute | solution.py:15
  15.2 10.3 %collective-permute-start.3 = (bf16[1,256]{1,0:T(2,128)(2,1)}, bf16[1,256]{1,0:T(2,128)(2,1)S(1)}, u32[]{:S(2)}, u32[]{:S(2)}) collective-permute-start(bf16[1,256]{1,0:T(2,128)(2,1)} %get-tuple-element.23), channel_id=1, source_target_pairs={{0,24},{8,0},{16,8},{24,16},{1,25},{9,1},{17,9},{25,17},{2,26},{10... | collective-permute-start | bytes 1544 | tf_op jit(solution)/shard_map/ppermute | solution.py:15
  15.2 10.3 %collective-permute-start.2 = (bf16[1,256]{1,0:T(2,128)(2,1)}, bf16[1,256]{1,0:T(2,128)(2,1)S(1)}, u32[]{:S(2)}, u32[]{:S(2)}) collective-permute-start(bf16[1,256]{1,0:T(2,128)(2,1)} %get-tuple-element.22), channel_id=1, source_target_pairs={{0,8},{8,16},{16,24},{24,0},{1,9},{9,17},{17,25},{25,1},{2,10},{10... | collective-permute-start | bytes 1544 | tf_op jit(solution)/shard_map/ppermute | solution.py:15
  16.5 41.4 %all-to-all-start.1 = ((bf16[2,1,256]{0,1,2:T(2,128)(2,1)}), bf16[2,1,256]{0,1,2:T(2,128)(2,1)S(1)}, u32[]{:S(2)}, u32[]{:S(2)}) async-start(bf16[2,1,256]{0,1,2:T(2,128)(2,1)} %copy.70), calls=%async_computation.1 | async-start | bytes 262144 | tf_op jit(solution)/shard_map/all_to_all | solution.py:114
  23.6 8.2 %copy-start.9 = (bf16[1,1,256,576]{2,3,0,1:T(8,128)(2,1)S(1)}, bf16[1,1,256,576]{2,3,0,1:T(8,128)(2,1)}, u32[]{:S(2)}) copy-start(bf16[1,1,256,576]{2,3,0,1:T(8,128)(2,1)} %get-tuple-element.16) | copy-start | bytes 884740
  23.6 8.5 %copy-start.3 = (bf16[2,1,256,576]{2,3,0,1:T(8,128)(2,1)S(1)}, bf16[2,1,256,576]{2,3,0,1:T(8,128)(2,1)}, u32[]{:S(2)}) copy-start(bf16[2,1,256,576]{2,3,0,1:T(8,128)(2,1)} %get-tuple-element.10) | copy-start | bytes 1769476
  23.6 8.5 %copy-start.4 = (bf16[2,1,256,576]{2,3,0,1:T(8,128)(2,1)S(1)}, bf16[2,1,256,576]{2,3,0,1:T(8,128)(2,1)}, u32[]{:S(2)}) copy-start(bf16[2,1,256,576]{2,3,0,1:T(8,128)(2,1)} %get-tuple-element.11) | copy-start | bytes 1769476
  25.5 6.4 %collective-permute-start.4 = (bf16[1,256,576]{1,2,0:T(8,128)(2,1)}, bf16[1,256,576]{1,2,0:T(8,128)(2,1)S(1)}, u32[]{:S(2)}, u32[]{:S(2)}) collective-permute-start(bf16[1,256,576]{1,2,0:T(8,128)(2,1)} %get-tuple-element.12), channel_id=1, source_target_pairs={{0,8},{8,16},{16,24},{24,0},{1,9},{9,17},{17,25},{25,1},{2,10},{10... | collective-permute-start | bytes 884744 | tf_op jit(solution)/shard_map/ppermute | solution.py:15
  33.9 7.0 %copy-start.5 = (bf16[2,1,256,576]{2,3,1,0:T(8,128)(2,1)S(1)}, bf16[2,1,256,576]{2,3,1,0:T(8,128)(2,1)}, u32[]{:S(2)}) copy-start(bf16[2,1,256,576]{2,3,1,0:T(8,128)(2,1)} %slice.72) | copy-start | bytes 1769476
  33.9 7.0 %copy-start.6 = (bf16[1,1,256,576]{2,3,1,0:T(8,128)(2,1)S(1)}, bf16[1,1,256,576]{2,3,1,0:T(8,128)(2,1)}, u32[]{:S(2)}) copy-start(bf16[1,1,256,576]{2,3,1,0:T(8,128)(2,1)} %get-tuple-element.15) | copy-start | bytes 884740
  42.1 6.8 %copy-start.2 = (bf16[2,1,256,1152]{3,2,1,0:T(8,128)(2,1)S(1)}, bf16[2,1,256,1152]{3,2,1,0:T(8,128)(2,1)}, u32[]{:S(2)}) copy-start(bf16[2,1,256,1152]{3,2,1,0:T(8,128)(2,1)} %param.8) | copy-start | bytes 3538948
  49.0 2.4 %copy-start.11 = (bf16[1152,1728]{0,1:T(8,128)(2,1)S(1)}, bf16[1152,1728]{0,1:T(8,128)(2,1)}, u32[]{:S(2)}) copy-start(bf16[1152,1728]{0,1:T(8,128)(2,1)} %param.14) | copy-start | bytes 11943940
  50.4 1.0 copy-start.7
  57.8 47.3 %all-to-all-start = ((bf16[2,1,256,1728]{3,0,1,2:T(2,128)(2,1)}), bf16[2,1,256,1728]{3,0,1,2:T(2,128)(2,1)S(1)}, u32[]{:S(2)}, u32[]{:S(2)}) async-start(bf16[2,1,256,1728]{3,0,1,2:T(2,128)(2,1)} %copy.68), calls=%async_computation | async-start | bytes 3670016 | tf_op jit(solution)/shard_map/all_to_all | solution.py:113
  119.6 21.2 %copy-start.8 = (bf16[2,1,256,1152]{3,2,0,1:T(8,128)(2,1)S(1)}, bf16[2,1,256,1152]{3,2,0,1:T(8,128)(2,1)}, u32[]{:S(2)}) copy-start(bf16[2,1,256,1152]{3,2,0,1:T(8,128)(2,1)} %copy-done.7) | copy-start | bytes 3538948
  119.6 21.2 %copy-start.12 = (bf16[576,1152]{1,0:T(8,128)(2,1)S(1)}, bf16[576,1152]{1,0:T(8,128)(2,1)}, u32[]{:S(2)}) copy-start(bf16[576,1152]{1,0:T(8,128)(2,1)} %param.15) | copy-start | bytes 3981316
where the time goes:
time: 143 us
  waiting for transfers between devices  45.9 us (32%)
  matrix products  27.5 us (19%)
  blocking collectives  21.1 us (15%)
  local copies, waits for them, and re-layouts  16.9 us (12%)
  starting transfers between devices  16.5 us (12%)
  other arithmetic  14.8 us (10%)
    all_to_all x1, waiting for transfers between devices, shards(): lax.all_to_all(time_proj, 'frame', split_axis=2, concat_axis=1, tiled=True)  40.8 us
    all_to_all x1, blocking collectives, temporal_tail(): lax.all_to_all(attended, 'frame', split_axis=1, concat_axis=2, tiled=True)  21.1 us
    dot_general x4, matrix products, project(): result = jnp.dot(flat, weight, preferred_element_type=jnp.float32)  11.2 us
    sub x1, other arithmetic, softmax_rows(): expo = jnp.exp(masked - highest)  7.01 us
    dot_general x1, matrix products, shards(): jnp.einsum('bhqk,bkhd->bqhd', probs, value_heads, preferred_element_type=...  6.82 us
    all_to_all x1, starting transfers between devices, shards(): lax.all_to_all(time_proj, 'frame', split_axis=2, concat_axis=1, tiled=True)  6 us
    all_to_all x1, starting transfers between devices, shards(): lax.all_to_all(valid, 'frame', split_axis=2, concat_axis=1, tiled=True)  5.81 us
    sub x1, matrix products, softmax_rows(): expo = jnp.exp(masked - highest)  5.12 us
  transfers between devices with their start and end apart: 8, of which 2 were waited for; matrix products, arithmetic and copies ran while one was open for 23% of the time, Pallas kernels for 0%

commit v1 on v0

--- a/solution.py
+++ b/solution.py
@@ -1,18 +1,19 @@
+import functools
+import math
+
 import jax
 import jax.numpy as jnp
 from jax import lax
+from jax.experimental import pallas as pl
+from jax.experimental.pallas import tpu as pltpu
 from jax.sharding import PartitionSpec as P
 
 HEADS = 8
-
+MESH = pl.DeviceIdType.MESH
 
 epsilon = 1e-06
 row_tokens = 64
-
-
-def passed_along(x, axis, by):
-    peers = lax.axis_size(axis)
-    return lax.ppermute(x, axis, [(i, (i + by) % peers) for i in range(peers)])
+minus = -1e30
 
 
 def normalize(values):
@@ -21,6 +22,436 @@
     centred = values - mean
     variance = jnp.mean(centred * centred, axis=-1, keepdims=True)
     return (centred * lax.rsqrt(variance + epsilon)).astype(jnp.bfloat16)
+
+
+def dot(a, b):
+    return jnp.dot(a, b, preferred_element_type=jnp.float32)
+
+
+def dot_t(a, b):
+    return lax.dot_general(a, b, (((1,), (1,)), ((), ())), preferred_element_type=jnp.float32)
+
+
+class Heads:
+    def __init__(self, inner):
+        self.inner = inner
+        self.size = inner // HEADS
+        self.scale = self.size ** (-0.5) * math.log2(math.e)
+        self.windows = []
+        for h in range(HEADS):
+            lo = h * self.size
+            start = lo // 128 * 128
+            end = min(-(-(lo + self.size) // 128) * 128, inner)
+            self.windows.append((start, end))
+
+    def mask(self, h, dtype):
+        start, end = self.windows[h]
+        lane = lax.broadcasted_iota(jnp.int32, (1, end - start), 1) + start
+        inside = (lane >= h * self.size) & (lane < (h + 1) * self.size)
+        return jnp.where(inside, 1.0, 0.0).astype(dtype)
+
+    def gather(self, results):
+        tiles = {}
+        for h, result in enumerate(results):
+            start, end = self.windows[h]
+            for at in range(start, end, 128):
+                piece = result[:, at - start : min(at + 128, end) - start]
+                tiles[at] = tiles[at] + piece if at in tiles else piece
+        return jnp.concatenate([tiles[at] for at in sorted(tiles)], axis=1)
+
+
+def block_kernel(
+    peers,
+    cam_peers,
+    counts,
+    neighbours,
+    tokens_hbm,
+    side_keys,
+    cross_qkv_hbm,
+    cross_out_hbm,
+    time_qkv_hbm,
+    time_out_hbm,
+    out,
+    tokens,
+    cross_qkv,
+    cross_out,
+    time_qkv,
+    time_out,
+    edge,
+    query,
+    keys,
+    values,
+    shifted,
+    sides,
+    far_values,
+    part,
+    highest,
+    total,
+    mixed,
+    leaving,
+    arrived,
+    attended,
+    returned,
+    count_out,
+    count_in,
+    count_edge,
+    load_sem,
+    edge_send,
+    edge_recv,
+    count_send,
+    count_recv,
+    cedge_send,
+    cedge_recv,
+    go_send,
+    go_recv,
+    back_send,
+    back_recv,
+):
+    cams, token_count, width = tokens.shape
+    inner = cross_out.shape[0]
+    heads = Heads(inner)
+    rows = token_count // peers
+    me = lax.axis_index("frame")
+    cam = lax.axis_index("cam")
+    above = lax.rem(cam + 1, cam_peers)
+    below = lax.rem(cam + cam_peers - 1, cam_peers)
+    others = [lax.rem(me + k, peers) for k in range(1, peers)]
+
+    loads = [
+        pltpu.make_async_copy(source, target, load_sem.at[i])
+        for i, (source, target) in enumerate(
+            (
+                (tokens_hbm, tokens),
+                (cross_qkv_hbm, cross_qkv),
+                (cross_out_hbm, cross_out),
+                (time_qkv_hbm, time_qkv),
+                (time_out_hbm, time_out),
+            )
+        )
+    ]
+    for load in loads:
+        load.start()
+
+    for c in range(cams):
+        count_out[pl.ds(c, 1), :] = jnp.full((1, token_count), counts[c, 0], jnp.int32)
+
+    barrier = pltpu.get_barrier_semaphore()
+    for peer in others:
+        pl.semaphore_signal(barrier, inc=1, device_id={"frame": peer}, device_id_type=MESH)
+    for peer in (above, below):
+        pl.semaphore_signal(barrier, inc=1, device_id={"cam": peer}, device_id_type=MESH)
+    pl.semaphore_wait(barrier, peers + 1)
+
+    def remote(source, target, send, recv, device):
+        return pltpu.make_async_remote_copy(
+            src_ref=source,
+            dst_ref=target,
+            send_sem=send,
+            recv_sem=recv,
+            device_id=device,
+            device_id_type=MESH,
+        )
+
+    edges = []
+    for slot, peer in ((0, above), (1, below)):
+        copy = remote(
+            tokens_hbm.at[1 - slot],
+            edge.at[slot],
+            edge_send.at[slot],
+            edge_recv.at[slot],
+            {"cam": peer},
+        )
+        copy.start()
+        edges.append(copy)
+    for slot, peer in ((0, above), (1, below)):
+        copy = remote(
+            count_out,
+            count_edge.at[slot],
+            cedge_send.at[slot],
+            cedge_recv.at[slot],
+            {"cam": peer},
+        )
+        copy.start()
+        edges.append(copy)
+
+    def count_copy(peer):
+        return remote(
+            count_out, count_in.at[me], count_send.at[peer], count_recv.at[me], {"frame": peer}
+        )
+
+    for peer in others:
+        count_copy(peer).start()
+    count_in[me] = count_out[...]
+
+    cameras = cams * cam_peers
+    first = side_keys[0:1, :].astype(jnp.float32)
+    second = side_keys[1:2, :].astype(jnp.float32)
+    for c in range(cams):
+        lower = lax.rem(cams * cam + c + cameras - 1, cameras)
+        straight = jnp.where(neighbours[c, 0] == lower, 1.0, 0.0)
+        side_lower = first * straight + second * (1.0 - straight)
+        side_upper = second * straight + first * (1.0 - straight)
+        near, far = (side_upper, side_lower) if c == 0 else (side_lower, side_upper)
+        sides[pl.ds(c, 1), :] = near
+        sides[pl.ds(cams + c, 1), :] = far
+
+    aligned = inner // 128 * 128
+
+    def key_value(normed, weight):
+        key = dot(normed, weight[:, aligned : 2 * inner])[:, inner - aligned :]
+        value = dot(normed, weight[:, 2 * inner :])
+        return key, value.astype(jnp.bfloat16)
+
+    loads[0].wait()
+    normed = normalize(tokens[...].reshape(cams * token_count, width))
+    loads[1].wait()
+    shape = (cams, token_count, inner)
+    query[...] = dot(normed, cross_qkv[:, :inner]).astype(jnp.bfloat16).reshape(shape)
+    key, value = key_value(normed, cross_qkv)
+    keys[...] = key.astype(jnp.bfloat16).reshape(shape)
+    values[...] = value.reshape(shape)
+
+    def bias_of(row):
+        lane = lax.broadcasted_iota(jnp.int32, row.shape, 1)
+        return jnp.where(lane < row_tokens * row, 0.0, minus)
+
+    def with_side(key, side):
+        return (key.astype(jnp.float32) + side).astype(jnp.bfloat16)
+
+    def local_part(c, carry):
+        near = 1 - c
+        shifted[...] = with_side(keys[near], sides[pl.ds(c, 1), :])
+        own_bias = bias_of(count_out[pl.ds(c, 1), :])
+        near_bias = bias_of(count_out[pl.ds(near, 1), :])
+        for h in range(HEADS):
+            start, end = heads.windows[h]
+            q = query[c, :, start:end] * heads.mask(h, jnp.bfloat16)
+            own = dot_t(q, keys[c, :, start:end]) * heads.scale + own_bias
+            other = dot_t(q, shifted[:, start:end]) * heads.scale + near_bias
+            top = jnp.max(jnp.maximum(own, other), axis=1, keepdims=True)
+            own = jnp.exp2(own - top)
+            other = jnp.exp2(other - top)
+            highest[c, h] = top
+            total[c, h] = jnp.sum(own + other, axis=1, keepdims=True)
+            part[c, h, :, : end - start] = dot(
+                own.astype(jnp.bfloat16), values[c, :, start:end]
+            ) + dot(other.astype(jnp.bfloat16), values[near, :, start:end])
+        return carry
+
+    lax.fori_loop(0, cams, local_part, 0)
+
+    def go_copy(c, peer):
+        return remote(
+            leaving.at[c, peer],
+            arrived.at[c, me],
+            go_send.at[c, peer],
+            go_recv.at[c, me],
+            {"frame": peer},
+        )
+
+    def back_copy(c, peer):
+        return remote(
+            attended.at[c, peer],
+            returned.at[c, me],
+            back_send.at[c, peer],
+            back_recv.at[c, me],
+            {"frame": peer},
+        )
+
+    def landed(buffer, sem, c, peer):
+        remote(
+            buffer.at[c, peer], buffer.at[c, peer], sem.at[c, peer], sem.at[c, peer], {"frame": peer}
+        ).wait_recv()
+
+    def camera_at(step):
+        return lax.rem(step + cam + 1, 2)
+
+    loads[2].wait()
+
+    def remote_part(step, carry):
+        c = camera_at(step)
+        remote(
+            edge.at[c], edge.at[c], edge_recv.at[c], edge_recv.at[c], {"cam": above}
+        ).wait_recv()
+        remote(
+            count_edge.at[c], count_edge.at[c], cedge_recv.at[c], cedge_recv.at[c], {"cam": above}
+        ).wait_recv()
+        key, value = key_value(normalize(edge[c]), cross_qkv)
+        shifted[...] = with_side(key.astype(jnp.bfloat16), sides[pl.ds(cams + c, 1), :])
+        far_values[...] = value
+        bias = bias_of(count_edge[c, pl.ds(1 - c, 1), :])
+        results = []
+        for h in range(HEADS):
+            start, end = heads.windows[h]
+            q = query[c, :, start:end] * heads.mask(h, jnp.bfloat16)
+            scores = dot_t(q, shifted[:, start:end]) * heads.scale + bias
+            before = highest[c, h]
+            top = jnp.maximum(before, jnp.max(scores, axis=1, keepdims=True))
+            scores = jnp.exp2(scores - top)
+            shrink = jnp.exp2(before - top)
+            whole = total[c, h] * shrink + jnp.sum(scores, axis=1, keepdims=True)
+            result = part[c, h, :, : end - start] * shrink + dot(
+                scores.astype(jnp.bfloat16), far_values[:, start:end]
+            )
+            results.append(result * (1.0 / whole) * heads.mask(h, jnp.float32))
+        result = heads.gather(results).astype(jnp.bfloat16)
+        sum_ = (dot(result, cross_out[...]) + tokens[c].astype(jnp.float32)).astype(jnp.bfloat16)
+        mixed[c] = sum_
+        leaving[c] = normalize(sum_).reshape(peers, rows, width)
+        for peer in others:
+            go_copy(c, peer).start()
+        arrived[c, me] = leaving[c, me]
+        return carry
+
+    lax.fori_loop(0, cams, remote_part, 0)
+
+    for peer in others:
+        remote(
+            count_in.at[peer],
+            count_in.at[peer],
+            count_recv.at[peer],
+            count_recv.at[peer],
+            {"frame": peer},
+        ).wait_recv()
+    loads[3].wait()
+
+    def time_part(step, carry):
+        c = camera_at(step)
+        row = lax.broadcasted_iota(jnp.int32, (token_count, 1), 0)
+        lane = lax.broadcasted_iota(jnp.int32, (1, token_count), 1)
+        count = jnp.zeros((1, token_count), jnp.int32)
+        row_frame = jnp.zeros((token_count, 1), jnp.int32)
+        lane_frame = jnp.zeros((1, token_count), jnp.int32)
+        for g in range(peers):
+            here = (lane >= g * rows) & (lane < (g + 1) * rows)
+            count = jnp.where(here, count_in[g, pl.ds(c, 1), :], count)
+            if g:
+                row_frame = row_frame + jnp.where(row >= g * rows, 1, 0)
+                lane_frame = lane_frame + jnp.where(lane >= g * rows, 1, 0)
+        place = lane - lane_frame * rows
+        valid = jnp.where(me * rows + place < row_tokens * count, 1, 0)
+        same_place = (row - row_frame * rows) == place
+        seen = jnp.where(row_frame == lane_frame, 1, valid)
+        bias = jnp.where(same_place, jnp.where(seen == 1, 0.0, minus), minus)
+        for peer in others:
+            landed(arrived, go_recv, c, peer)
+        x = arrived[c].reshape(token_count, width)
+        query[0] = dot(x, time_qkv[:, :inner]).astype(jnp.bfloat16)
+        key, value = key_value(x, time_qkv)
+        keys[0] = key.astype(jnp.bfloat16)
+        values[0] = value
+        results = []
+        for h in range(HEADS):
+            start, end = heads.windows[h]
+            q = query[0, :, start:end] * heads.mask(h, jnp.bfloat16)
+            scores = dot_t(q, keys[0, :, start:end]) * heads.scale + bias
+            scores = jnp.exp2(scores - jnp.max(scores, axis=1, keepdims=True))
+            whole = jnp.sum(scores, axis=1, keepdims=True)
+            result = dot(scores.astype(jnp.bfloat16), values[0, :, start:end])
+            results.append(result * (1.0 / whole) * heads.mask(h, jnp.float32))
+        result = heads.gather(results).astype(jnp.bfloat16)
+        attended[c] = result.reshape(peers, rows, inner)
+        for peer in others:
+            back_copy(c, peer).start()
+        returned[c, me] = attended[c, me]
+        return carry
+
+    lax.fori_loop(0, cams, time_part, 0)
+    loads[4].wait()
+
+    def last_part(step, carry):
+        c = camera_at(step)
+        for peer in others:
+            landed(returned, back_recv, c, peer)
+        x = returned[c].reshape(token_count, inner)
+        out[c] = (dot(x, time_out[...]) + mixed[c].astype(jnp.float32)).astype(jnp.bfloat16)
+        return carry
+
+    lax.fori_loop(0, cams, last_part, 0)
+
+    for copy in edges:
+        copy.wait_send()
+    for peer in others:
+        count_copy(peer).wait_send()
+        for c in range(cams):
+            go_copy(c, peer).wait_send()
+            back_copy(c, peer).wait_send()
+
+
+def whole_block(
+    tokens, counts, neighbours, side_keys, cross_qkv, cross_out, time_qkv, time_out
+):
+    cams, frames, token_count, width = tokens.shape
+    inner = cross_out.shape[0]
+    peers = lax.axis_size("frame")
+    cam_peers = lax.axis_size("cam")
+    rows = token_count // peers
+    bf16, f32 = jnp.bfloat16, jnp.float32
+    vmem, smem, hbm = (
+        pl.BlockSpec(memory_space=space) for space in (pltpu.VMEM, pltpu.SMEM, pl.ANY)
+    )
+    dma = pltpu.SemaphoreType.DMA
+    scratch = [
+        pltpu.VMEM((cams, token_count, width), bf16),
+        pltpu.VMEM(cross_qkv.shape, bf16),
+        pltpu.VMEM(cross_out.shape, bf16),
+        pltpu.VMEM(time_qkv.shape, bf16),
+        pltpu.VMEM(time_out.shape, bf16),
+        pltpu.VMEM((2, token_count, width), bf16),
+        pltpu.VMEM((cams, token_count, inner), bf16),
+        pltpu.VMEM((cams, token_count, inner), bf16),
+        pltpu.VMEM((cams, token_count, inner), bf16),
+        pltpu.VMEM((token_count, inner), bf16),
+        pltpu.VMEM((8, inner), f32),
+        pltpu.VMEM((token_count, inner), bf16),
+        pltpu.VMEM((cams, HEADS, token_count, 256), f32),
+        pltpu.VMEM((cams, HEADS, token_count, 1), f32),
+        pltpu.VMEM((cams, HEADS, token_count, 1), f32),
+        pltpu.VMEM((cams, token_count, width), bf16),
+        pltpu.VMEM((cams, peers, rows, width), bf16),
+        pltpu.VMEM((cams, peers, rows, width), bf16),
+        pltpu.VMEM((cams, peers, rows, inner), bf16),
+        pltpu.VMEM((cams, peers, rows, inner), bf16),
+        pltpu.VMEM((8, token_count), jnp.int32),
+        pltpu.VMEM((peers, 8, token_count), jnp.int32),
+        pltpu.VMEM((2, 8, token_count), jnp.int32),
+        dma((5,)),
+        dma((2,)),
+        dma((2,)),
+        dma((peers,)),
+        dma((peers,)),
+        dma((2,)),
+        dma((2,)),
+        dma((cams, peers)),
+        dma((cams, peers)),
+        dma((cams, peers)),
+        dma((cams, peers)),
+    ]
+    result = pl.pallas_call(
+        functools.partial(block_kernel, peers, cam_peers),
+        out_shape=jax.ShapeDtypeStruct((cams, token_count, width), bf16),
+        in_specs=[smem, smem, hbm, vmem, hbm, hbm, hbm, hbm],
+        out_specs=vmem,
+        scratch_shapes=scratch,
+        compiler_params=pltpu.CompilerParams(
+            collective_id=0, has_side_effects=True, vmem_limit_bytes=58 * 2**20
+        ),
+    )(
+        counts,
+        neighbours,
+        tokens.reshape(cams, token_count, width),
+        side_keys,
+        cross_qkv,
+        cross_out,
+        time_qkv,
+        time_out,
+    )
+    return result.reshape(tokens.shape)
+
+
+def passed_along(x, axis, by):
+    peers = lax.axis_size(axis)
+    return lax.ppermute(x, axis, [(i, (i + by) % peers) for i in range(peers)])
 
 
 def project(normed, weight):
@@ -59,7 +490,7 @@
     return project(returned, time_out)
 
 
-def shards(tokens, counts, neighbours, side_keys, cross_qkv, cross_out, time_qkv, time_out):
+def plain_block(tokens, counts, neighbours, side_keys, cross_qkv, cross_out, time_qkv, time_out):
     cam_here, frames_here, token_count, width = tokens.shape
     inner = cross_out.shape[0]
     head_size = inner // HEADS
@@ -107,14 +538,29 @@
     attended = jnp.einsum("bhqk,bkhd->bqhd", probs, value_heads, preferred_element_type=jnp.float32)
     attended = attended.astype(jnp.bfloat16).reshape(cam_here, frames_here, token_count, inner)
     mixed = (project(attended, cross_out) + tokens.astype(jnp.float32)).astype(jnp.bfloat16)
-    normed = normalize(mixed)
-    time_proj = project(normed, time_qkv).astype(jnp.bfloat16)
+    normed = lax.all_to_all(normalize(mixed), "frame", split_axis=2, concat_axis=1, tiled=True)
     temporal = temporal_tail(
-        lax.all_to_all(time_proj, "frame", split_axis=2, concat_axis=1, tiled=True),
+        project(normed, time_qkv).astype(jnp.bfloat16),
         lax.all_to_all(valid, "frame", split_axis=2, concat_axis=1, tiled=True),
         time_out,
     )
     return (temporal + mixed.astype(jnp.float32)).astype(jnp.bfloat16)
+
+
+def shards(tokens, counts, neighbours, side_keys, cross_qkv, cross_out, time_qkv, time_out):
+    cams, frames, token_count, _ = tokens.shape
+    peers = lax.axis_size("frame")
+    fits = (
+        cams == 2
+        and frames == 1
+        and lax.axis_size("cam") > 2
+        and token_count == 256
+        and token_count % (16 * peers) == 0
+    )
+    chosen = whole_block if fits else plain_block
+    return chosen(
+        tokens, counts, neighbours, side_keys, cross_qkv, cross_out, time_qkv, time_out
+    )
 
 
 def solution(mesh):

time: 143 us -> 83.8 us (0.59)
  Pallas kernels: 0 us -> 66.8 us
  waiting for transfers between devices: 45.9 us -> 0 us
  matrix products: 27.5 us -> 0 us
  blocking collectives: 21.1 us -> 0 us
  starting transfers between devices: 16.5 us -> 0 us
  other arithmetic: 14.8 us -> 0 us
    pallas_call x0 -> x1, Pallas kernels: none -> 66.8 us  [whole_block(): pl.pallas_call(functools.partial(block_kernel, peers, cam_peers), out_sha...]
    all_to_all x2 -> x0, waiting for transfers between devices: 40.8 us -> none  [the longest x1 40.8 us: shards(): lax.all_to_all(time_proj, 'frame', split_axis=2, concat_axis=1, tiled=True)]
    dot_general x7 -> x0, matrix products: 22.4 us -> none  [the longest x4 11.2 us: project(): result = jnp.dot(flat, weight, preferred_element_type=jnp.float32)]
    all_to_all x1 -> x0, blocking collectives: 21.1 us -> none  [temporal_tail(): lax.all_to_all(attended, 'frame', split_axis=1, concat_axis=2, tiled=True)]
    unnamed x29 -> x4, local copies, waits for them, and re-layouts: 0.62 us -> 16.6 us
    all_to_all x2 -> x0, starting transfers between devices: 11.8 us -> none  [the longest x1 6 us: shards(): lax.all_to_all(time_proj, 'frame', split_axis=2, concat_axis=1, tiled=True)]
    sub x1 -> x0, other arithmetic: 7.01 us -> none  [softmax_rows(): expo = jnp.exp(masked - highest)]
    reshape x5 -> x0, local copies, waits for them, and re-layouts: 6.02 us -> none  [the longest x1 2.01 us: temporal_tail(): projected[..., inner:2 * inner]]
  transfers between devices with their start and end apart: 8 -> 0, of which waited for: 2 -> 0; matrix products, arithmetic and copies ran while one was open for 23% -> 0% of each run, Pallas kernels for 0% -> 0%
where the time goes in v1:
time: 83.8 us; the launch traced here: 83.4 us
  Pallas kernels  66.8 us (80%)
  local copies, waits for them, and re-layouts  16.6 us (20%)
    pallas_call x1, Pallas kernels, whole_block(): pl.pallas_call(functools.partial(block_kernel, peers, cam_peers), out_sha...  66.8 us
    unnamed x4, local copies, waits for them, and re-layouts  16.6 us

profile of v1, /device:TPU:0, one launch (start us, length us, event | category | flops | bytes accessed | tf_op | source)
XLA Modules:
  0.0 83.4 jit_solution(4076439499325504877)
XLA Ops:
  0.0 1.3 %copy.9.counts = s32[2,1]{1,0:T(2,128)} copy(s32[2,1]{0,1:T(1,128)} %param.9) | data formatting | bytes 16 | tf_op args[1]
  1.3 6.4 %copy.10.cross_qkv_hbm = bf16[1152,1728]{1,0:T(8,128)(2,1)} copy(bf16[1152,1728]{0,1:T(8,128)(2,1)} %param.12) | data formatting | bytes 7962624 | tf_op args[4]
  7.7 6.5 %copy.11.time_qkv_hbm = bf16[1152,1728]{1,0:T(8,128)(2,1)} copy(bf16[1152,1728]{0,1:T(8,128)(2,1)} %param.14) | data formatting | bytes 7962624 | tf_op args[6]
  14.2 66.8 %shard_map.82 = bf16[2,256,1152]{2,1,0:T(8,128)(2,1)} custom-call(s32[2,1]{1,0:T(2,128)} %copy.9.counts, s32[2,2]{1,0:T(2,128)} %neighbours.1, bf16[2,256,1152]{2,1,0:T(8,128)(2,1)} %bitcast.5, bf16[2,576]{1,0:T(2,128)(2,1)} %side_keys.1, bf16[1152,1728]{1,0:T(8,128)(2,1)} %copy.10.cross_qkv_hbm, bf16[576,1152]{1,0:T(8,128)(2,1)} %cross_out_hbm.1, ...), custom_call_target="tpu_custom_call" | custom-call | tf_op jit(solution)/shard_map/pallas_call | solution.py:430
  81.0 2.4 %copy.14 = bf16[2,1,256,1152]{3,2,1,0:T(8,128)(2,1)} copy(bf16[2,1,256,1152]{3,2,1,0:T(8,128)(2,1)} %bitcast.4) | data formatting | bytes 2359296

commit v2 on v1

--- a/solution.py
+++ b/solution.py
@@ -90,6 +90,10 @@
     mixed,
     leaving,
     arrived,
+    early,
+    crossed,
+    late,
+    incoming,
     attended,
     returned,
     count_out,
@@ -102,8 +106,12 @@
     count_recv,
     cedge_send,
     cedge_recv,
+    early_send,
+    early_recv,
     go_send,
     go_recv,
+    late_send,
+    late_recv,
     back_send,
     back_recv,
 ):
@@ -115,7 +123,13 @@
     cam = lax.axis_index("cam")
     above = lax.rem(cam + 1, cam_peers)
     below = lax.rem(cam + cam_peers - 1, cam_peers)
-    others = [lax.rem(me + k, peers) for k in range(1, peers)]
+    half = peers // 2
+    side, place_in = lax.div(me, half), lax.rem(me, half)
+    others = []
+    for k in range(half):
+        if k:
+            others.append(side * half + lax.rem(place_in + k, half))
+        others.append((1 - side) * half + lax.rem(place_in + k, half))
 
     loads = [
         pltpu.make_async_copy(source, target, load_sem.at[i])
@@ -133,7 +147,7 @@
         load.start()
 
     for c in range(cams):
-        count_out[pl.ds(c, 1), :] = jnp.full((1, token_count), counts[c, 0], jnp.int32)
+        count_out[pl.ds(c, 1), :] = jnp.full((1, token_count), counts[0, c], jnp.int32)
 
     barrier = pltpu.get_barrier_semaphore()
     for peer in others:
@@ -173,6 +187,21 @@
         )
         copy.start()
         edges.append(copy)
+
+    def camera_at(step):
+        return lax.rem(step + cam + 1, 2)
+
+    def early_copy(peer):
+        return remote(
+            tokens_hbm.at[camera_at(1), pl.ds(pl.multiple_of(peer * rows, rows), rows)],
+            early.at[me],
+            early_send.at[peer],
+            early_recv.at[me],
+            {"frame": peer},
+        )
+
+    for peer in others:
+        early_copy(peer).start()
 
     def count_copy(peer):
         return remote(
@@ -195,18 +224,16 @@
         sides[pl.ds(c, 1), :] = near
         sides[pl.ds(cams + c, 1), :] = far
 
-    aligned = inner // 128 * 128
-
     def key_value(normed, weight):
-        key = dot(normed, weight[:, aligned : 2 * inner])[:, inner - aligned :]
-        value = dot(normed, weight[:, 2 * inner :])
+        key = dot_t(normed, weight[inner : 2 * inner, :])
+        value = dot_t(normed, weight[2 * inner :, :])
         return key, value.astype(jnp.bfloat16)
 
     loads[0].wait()
     normed = normalize(tokens[...].reshape(cams * token_count, width))
     loads[1].wait()
     shape = (cams, token_count, inner)
-    query[...] = dot(normed, cross_qkv[:, :inner]).astype(jnp.bfloat16).reshape(shape)
+    query[...] = dot_t(normed, cross_qkv[:inner, :]).astype(jnp.bfloat16).reshape(shape)
     key, value = key_value(normed, cross_qkv)
     keys[...] = key.astype(jnp.bfloat16).reshape(shape)
     values[...] = value.reshape(shape)
@@ -218,7 +245,7 @@
     def with_side(key, side):
         return (key.astype(jnp.float32) + side).astype(jnp.bfloat16)
 
-    def local_part(c, carry):
+    def local_part(c):
         near = 1 - c
         shifted[...] = with_side(keys[near], sides[pl.ds(c, 1), :])
         own_bias = bias_of(count_out[pl.ds(c, 1), :])
@@ -236,17 +263,15 @@
             part[c, h, :, : end - start] = dot(
                 own.astype(jnp.bfloat16), values[c, :, start:end]
             ) + dot(other.astype(jnp.bfloat16), values[near, :, start:end])
-        return carry
-
-    lax.fori_loop(0, cams, local_part, 0)
-
-    def go_copy(c, peer):
+
+    def go_copy(peer):
         return remote(
-            leaving.at[c, peer],
-            arrived.at[c, me],
-            go_send.at[c, peer],
-            go_recv.at[c, me],
-            {"frame": peer},
+            leaving.at[peer], arrived.at[me], go_send.at[peer], go_recv.at[me], {"frame": peer}
+        )
+
+    def late_copy(peer):
+        return remote(
+            crossed.at[peer], late.at[me], late_send.at[peer], late_recv.at[me], {"frame": peer}
         )
 
     def back_copy(c, peer):
@@ -258,18 +283,14 @@
             {"frame": peer},
         )
 
-    def landed(buffer, sem, c, peer):
-        remote(
-            buffer.at[c, peer], buffer.at[c, peer], sem.at[c, peer], sem.at[c, peer], {"frame": peer}
-        ).wait_recv()
-
-    def camera_at(step):
-        return lax.rem(step + cam + 1, 2)
+    def landed(buffer, sem, *at):
+        remote(buffer.at[at], buffer.at[at], sem.at[at], sem.at[at], {"frame": at[-1]}).wait_recv()
 
     loads[2].wait()
 
-    def remote_part(step, carry):
+    def cross_part(step, carry):
         c = camera_at(step)
+        local_part(c)
         remote(
             edge.at[c], edge.at[c], edge_recv.at[c], edge_recv.at[c], {"cam": above}
         ).wait_recv()
@@ -297,13 +318,25 @@
         result = heads.gather(results).astype(jnp.bfloat16)
         sum_ = (dot(result, cross_out[...]) + tokens[c].astype(jnp.float32)).astype(jnp.bfloat16)
         mixed[c] = sum_
-        leaving[c] = normalize(sum_).reshape(peers, rows, width)
-        for peer in others:
-            go_copy(c, peer).start()
-        arrived[c, me] = leaving[c, me]
+
+        @pl.when(step == 0)
+        def _():
+            leaving[...] = normalize(sum_).reshape(peers, rows, width)
+            for peer in others:
+                go_copy(peer).start()
+            arrived[me] = leaving[me]
+
+        @pl.when(step == 1)
+        def _():
+            crossed[...] = result.reshape(peers, rows, inner)
+            for peer in others:
+                late_copy(peer).start()
+            late[me] = crossed[me]
+            early[me] = tokens[c, pl.ds(pl.multiple_of(me * rows, rows), rows), :]
+
         return carry
 
-    lax.fori_loop(0, cams, remote_part, 0)
+    lax.fori_loop(0, cams, cross_part, 0)
 
     for peer in others:
         remote(
@@ -333,10 +366,24 @@
         same_place = (row - row_frame * rows) == place
         seen = jnp.where(row_frame == lane_frame, 1, valid)
         bias = jnp.where(same_place, jnp.where(seen == 1, 0.0, minus), minus)
-        for peer in others:
-            landed(arrived, go_recv, c, peer)
-        x = arrived[c].reshape(token_count, width)
-        query[0] = dot(x, time_qkv[:, :inner]).astype(jnp.bfloat16)
+
+        @pl.when(step == 0)
+        def _():
+            for peer in others:
+                landed(arrived, go_recv, peer)
+            incoming[...] = arrived[...].reshape(token_count, width)
+
+        @pl.when(step == 1)
+        def _():
+            for peer in others:
+                landed(early, early_recv, peer)
+                landed(late, late_recv, peer)
+            again = dot(late[...].reshape(token_count, inner), cross_out[...])
+            again = again + early[...].reshape(token_count, width).astype(jnp.float32)
+            incoming[...] = normalize(again.astype(jnp.bfloat16))
+
+        x = incoming[...]
+        query[0] = dot_t(x, time_qkv[:inner, :]).astype(jnp.bfloat16)
         key, value = key_value(x, time_qkv)
         keys[0] = key.astype(jnp.bfloat16)
         values[0] = value
@@ -373,8 +420,10 @@
         copy.wait_send()
     for peer in others:
         count_copy(peer).wait_send()
+        early_copy(peer).wait_send()
+        go_copy(peer).wait_send()
+        late_copy(peer).wait_send()
         for c in range(cams):
-            go_copy(c, peer).wait_send()
             back_copy(c, peer).wait_send()
 
 
@@ -393,9 +442,9 @@
     dma = pltpu.SemaphoreType.DMA
     scratch = [
         pltpu.VMEM((cams, token_count, width), bf16),
-        pltpu.VMEM(cross_qkv.shape, bf16),
+        pltpu.VMEM(cross_qkv.shape[::-1], bf16),
         pltpu.VMEM(cross_out.shape, bf16),
-        pltpu.VMEM(time_qkv.shape, bf16),
+        pltpu.VMEM(time_qkv.shape[::-1], bf16),
         pltpu.VMEM(time_out.shape, bf16),
         pltpu.VMEM((2, token_count, width), bf16),
         pltpu.VMEM((cams, token_count, inner), bf16),
@@ -408,8 +457,12 @@
         pltpu.VMEM((cams, HEADS, token_count, 1), f32),
         pltpu.VMEM((cams, HEADS, token_count, 1), f32),
         pltpu.VMEM((cams, token_count, width), bf16),
-        pltpu.VMEM((cams, peers, rows, width), bf16),
-        pltpu.VMEM((cams, peers, rows, width), bf16),
+        pltpu.VMEM((peers, rows, width), bf16),
+        pltpu.VMEM((peers, rows, width), bf16),
+        pltpu.VMEM((peers, rows, width), bf16),
+        pltpu.VMEM((peers, rows, inner), bf16),
+        pltpu.VMEM((peers, rows, inner), bf16),
+        pltpu.VMEM((token_count, width), bf16),
         pltpu.VMEM((cams, peers, rows, inner), bf16),
         pltpu.VMEM((cams, peers, rows, inner), bf16),
         pltpu.VMEM((8, token_count), jnp.int32),
@@ -422,8 +475,12 @@
         dma((peers,)),
         dma((2,)),
         dma((2,)),
-        dma((cams, peers)),
-        dma((cams, peers)),
+        dma((peers,)),
+        dma((peers,)),
+        dma((peers,)),
+        dma((peers,)),
+        dma((peers,)),
+        dma((peers,)),
         dma((cams, peers)),
         dma((cams, peers)),
     ]
@@ -437,13 +494,13 @@
             collective_id=0, has_side_effects=True, vmem_limit_bytes=58 * 2**20
         ),
     )(
-        counts,
+        counts.T,
         neighbours,
         tokens.reshape(cams, token_count, width),
         side_keys,
-        cross_qkv,
+        cross_qkv.T,
         cross_out,
-        time_qkv,
+        time_qkv.T,
         time_out,
     )
     return result.reshape(tokens.shape)

time: 83.8 us -> 61.6 us (0.74)
  local copies, waits for them, and re-layouts: 16.6 us -> 2.37 us
  Pallas kernels: 66.8 us -> 59 us
    unnamed x4 -> x1, local copies, waits for them, and re-layouts: 16.6 us -> 2.37 us
    pallas_call x1, Pallas kernels: 66.8 us -> 59 us  [whole_block(): pl.pallas_call(functools.partial(block_kernel, peers, cam_peers), out_sha...]
where the time goes in v2:
time: 61.6 us; the launch traced here: 61.4 us
  Pallas kernels  59 us (96%)
  local copies, waits for them, and re-layouts  2.37 us (4%)
    pallas_call x1, Pallas kernels, whole_block(): pl.pallas_call(functools.partial(block_kernel, peers, cam_peers), out_sha...  59 us
    unnamed x1, local copies, waits for them, and re-layouts  2.37 us

profile of v2, /device:TPU:0, one launch (start us, length us, event | category | flops | bytes accessed | tf_op | source)
XLA Modules:
  0.0 61.4 jit_solution(6728351849291379987)
XLA Ops:
  0.0 59.0 %shard_map.82 = bf16[2,256,1152]{2,1,0:T(8,128)(2,1)} custom-call(s32[1,2]{1,0:T(1,128)} %bitcast.11, s32[2,2]{1,0:T(2,128)} %neighbours.1, bf16[2,256,1152]{2,1,0:T(8,128)(2,1)} %bitcast.10, bf16[2,576]{1,0:T(2,128)(2,1)} %side_keys.1, bf16[1728,1152]{1,0:T(8,128)(2,1)} %bitcast.8, bf16[576,1152]{1,0:T(8,128)(2,1)} %cross_out_hbm.1, ...), custom_call_target="tpu_custom_call" | custom-call | tf_op jit(solution)/shard_map/pallas_call | solution.py:487
  59.0 2.4 %copy.11 = bf16[2,1,256,1152]{3,2,1,0:T(8,128)(2,1)} copy(bf16[2,1,256,1152]{3,2,1,0:T(8,128)(2,1)} %bitcast.7) | data formatting | bytes 2359296

commit v3 on v2

--- a/solution.py
+++ b/solution.py
@@ -84,9 +84,7 @@
     shifted,
     sides,
     far_values,
-    part,
-    highest,
-    total,
+    normal,
     mixed,
     leaving,
     arrived,
@@ -231,9 +229,9 @@
 
     loads[0].wait()
     normed = normalize(tokens[...].reshape(cams * token_count, width))
+    normal[...] = normed.reshape(cams, token_count, width)
     loads[1].wait()
     shape = (cams, token_count, inner)
-    query[...] = dot_t(normed, cross_qkv[:inner, :]).astype(jnp.bfloat16).reshape(shape)
     key, value = key_value(normed, cross_qkv)
     keys[...] = key.astype(jnp.bfloat16).reshape(shape)
     values[...] = value.reshape(shape)
@@ -244,25 +242,6 @@
 
     def with_side(key, side):
         return (key.astype(jnp.float32) + side).astype(jnp.bfloat16)
-
-    def local_part(c):
-        near = 1 - c
-        shifted[...] = with_side(keys[near], sides[pl.ds(c, 1), :])
-        own_bias = bias_of(count_out[pl.ds(c, 1), :])
-        near_bias = bias_of(count_out[pl.ds(near, 1), :])
-        for h in range(HEADS):
-            start, end = heads.windows[h]
-            q = query[c, :, start:end] * heads.mask(h, jnp.bfloat16)
-            own = dot_t(q, keys[c, :, start:end]) * heads.scale + own_bias
-            other = dot_t(q, shifted[:, start:end]) * heads.scale + near_bias
-            top = jnp.max(jnp.maximum(own, other), axis=1, keepdims=True)
-            own = jnp.exp2(own - top)
-            other = jnp.exp2(other - top)
-            highest[c, h] = top
-            total[c, h] = jnp.sum(own + other, axis=1, keepdims=True)
-            part[c, h, :, : end - start] = dot(
-                own.astype(jnp.bfloat16), values[c, :, start:end]
-            ) + dot(other.astype(jnp.bfloat16), values[near, :, start:end])
 
     def go_copy(peer):
         return remote(
@@ -290,7 +269,9 @@
 
     def cross_part(step, carry):
         c = camera_at(step)
-        local_part(c)
+        near = 1 - c
+        query[...] = dot_t(normal[c], cross_qkv[:inner, :]).astype(jnp.bfloat16)
+        shifted[0] = with_side(keys[near], sides[pl.ds(c, 1), :])
         remote(
             edge.at[c], edge.at[c], edge_recv.at[c], edge_recv.at[c], {"cam": above}
         ).wait_recv()
@@ -298,21 +279,30 @@
             count_edge.at[c], count_edge.at[c], cedge_recv.at[c], cedge_recv.at[c], {"cam": above}
         ).wait_recv()
         key, value = key_value(normalize(edge[c]), cross_qkv)
-        shifted[...] = with_side(key.astype(jnp.bfloat16), sides[pl.ds(cams + c, 1), :])
+        shifted[1] = with_side(key.astype(jnp.bfloat16), sides[pl.ds(cams + c, 1), :])
         far_values[...] = value
-        bias = bias_of(count_edge[c, pl.ds(1 - c, 1), :])
+        biases = (
+            bias_of(count_out[pl.ds(c, 1), :]),
+            bias_of(count_out[pl.ds(near, 1), :]),
+            bias_of(count_edge[c, pl.ds(near, 1), :]),
+        )
         results = []
         for h in range(HEADS):
             start, end = heads.windows[h]
-            q = query[c, :, start:end] * heads.mask(h, jnp.bfloat16)
-            scores = dot_t(q, shifted[:, start:end]) * heads.scale + bias
-            before = highest[c, h]
-            top = jnp.maximum(before, jnp.max(scores, axis=1, keepdims=True))
-            scores = jnp.exp2(scores - top)
-            shrink = jnp.exp2(before - top)
-            whole = total[c, h] * shrink + jnp.sum(scores, axis=1, keepdims=True)
-            result = part[c, h, :, : end - start] * shrink + dot(
-                scores.astype(jnp.bfloat16), far_values[:, start:end]
+            lanes = slice(start, end)
+            q = query[:, lanes] * heads.mask(h, jnp.bfloat16)
+            groups = (keys[c, :, lanes], shifted[0, :, lanes], shifted[1, :, lanes])
+            scores = [
+                dot_t(q, group) * heads.scale + bias for group, bias in zip(groups, biases)
+            ]
+            top = jnp.max(functools.reduce(jnp.maximum, scores), axis=1, keepdims=True)
+            scores = [jnp.exp2(score - top) for score in scores]
+            whole = jnp.sum(scores[0] + scores[1] + scores[2], axis=1, keepdims=True)
+            weights = [score.astype(jnp.bfloat16) for score in scores]
+            result = (
+                dot(weights[0], values[c, :, lanes])
+                + dot(weights[1], values[near, :, lanes])
+                + dot(weights[2], far_values[:, lanes])
             )
             results.append(result * (1.0 / whole) * heads.mask(h, jnp.float32))
         result = heads.gather(results).astype(jnp.bfloat16)
@@ -383,14 +373,14 @@
             incoming[...] = normalize(again.astype(jnp.bfloat16))
 
         x = incoming[...]
-        query[0] = dot_t(x, time_qkv[:inner, :]).astype(jnp.bfloat16)
+        query[...] = dot_t(x, time_qkv[:inner, :]).astype(jnp.bfloat16)
         key, value = key_value(x, time_qkv)
         keys[0] = key.astype(jnp.bfloat16)
         values[0] = value
         results = []
         for h in range(HEADS):
             start, end = heads.windows[h]
-            q = query[0, :, start:end] * heads.mask(h, jnp.bfloat16)
+            q = query[:, start:end] * heads.mask(h, jnp.bfloat16)
             scores = dot_t(q, keys[0, :, start:end]) * heads.scale + bias
             scores = jnp.exp2(scores - jnp.max(scores, axis=1, keepdims=True))
             whole = jnp.sum(scores, axis=1, keepdims=True)
@@ -447,15 +437,13 @@
         pltpu.VMEM(time_qkv.shape[::-1], bf16),
         pltpu.VMEM(time_out.shape, bf16),
         pltpu.VMEM((2, token_count, width), bf16),
+        pltpu.VMEM((token_count, inner), bf16),
         pltpu.VMEM((cams, token_count, inner), bf16),
         pltpu.VMEM((cams, token_count, inner), bf16),
-        pltpu.VMEM((cams, token_count, inner), bf16),
-        pltpu.VMEM((token_count, inner), bf16),
+        pltpu.VMEM((2, token_count, inner), bf16),
         pltpu.VMEM((8, inner), f32),
         pltpu.VMEM((token_count, inner), bf16),
-        pltpu.VMEM((cams, HEADS, token_count, 256), f32),
-        pltpu.VMEM((cams, HEADS, token_count, 1), f32),
-        pltpu.VMEM((cams, HEADS, token_count, 1), f32),
+        pltpu.VMEM((cams, token_count, width), bf16),
         pltpu.VMEM((cams, token_count, width), bf16),
         pltpu.VMEM((peers, rows, width), bf16),
         pltpu.VMEM((peers, rows, width), bf16),

time: 61.6 us -> 61.5 us (level)
  no operation moved by 1% of the time
where the time goes in v3:
time: 61.5 us; the launch traced here: 61.4 us
  Pallas kernels  59 us (96%)
  local copies, waits for them, and re-layouts  2.37 us (4%)
    pallas_call x1, Pallas kernels, whole_block(): pl.pallas_call(functools.partial(block_kernel, peers, cam_peers), out_sha...  59 us
    unnamed x1, local copies, waits for them, and re-layouts  2.37 us

profile of v3, /device:TPU:0, one launch (start us, length us, event | category | flops | bytes accessed | tf_op | source)
XLA Modules:
  0.0 61.4 jit_solution(14278707793266061708)
XLA Ops:
  0.0 59.0 %shard_map.82 = bf16[2,256,1152]{2,1,0:T(8,128)(2,1)} custom-call(s32[1,2]{1,0:T(1,128)} %bitcast.11, s32[2,2]{1,0:T(2,128)} %neighbours.1, bf16[2,256,1152]{2,1,0:T(8,128)(2,1)} %bitcast.10, bf16[2,576]{1,0:T(2,128)(2,1)} %side_keys.1, bf16[1728,1152]{1,0:T(8,128)(2,1)} %bitcast.8, bf16[576,1152]{1,0:T(8,128)(2,1)} %cross_out_hbm.1, ...), custom_call_target="tpu_custom_call" | custom-call | tf_op jit(solution)/shard_map/pallas_call | solution.py:475
  59.0 2.4 %copy.11 = bf16[2,1,256,1152]{3,2,1,0:T(8,128)(2,1)} copy(bf16[2,1,256,1152]{3,2,1,0:T(8,128)(2,1)} %bitcast.7) | data formatting | bytes 2359296

commit v4 on v3

--- a/solution.py
+++ b/solution.py
@@ -70,13 +70,12 @@
     cross_qkv_hbm,
     cross_out_hbm,
     time_qkv_hbm,
-    time_out_hbm,
-    out,
+    temporal_hbm,
+    mixed_hbm,
     tokens,
     cross_qkv,
     cross_out,
     time_qkv,
-    time_out,
     edge,
     query,
     keys,
@@ -98,6 +97,7 @@
     count_in,
     count_edge,
     load_sem,
+    store_sem,
     edge_send,
     edge_recv,
     count_send,
@@ -137,7 +137,6 @@
                 (cross_qkv_hbm, cross_qkv),
                 (cross_out_hbm, cross_out),
                 (time_qkv_hbm, time_qkv),
-                (time_out_hbm, time_out),
             )
         )
     ]
@@ -242,6 +241,12 @@
 
     def with_side(key, side):
         return (key.astype(jnp.float32) + side).astype(jnp.bfloat16)
+
+    def mixed_store(c):
+        return pltpu.make_async_copy(mixed.at[c], mixed_hbm.at[c], store_sem.at[c])
+
+    def temporal_store(c):
+        return pltpu.make_async_copy(returned.at[c], temporal_hbm.at[c], store_sem.at[cams + c])
 
     def go_copy(peer):
         return remote(
@@ -308,6 +313,7 @@
         result = heads.gather(results).astype(jnp.bfloat16)
         sum_ = (dot(result, cross_out[...]) + tokens[c].astype(jnp.float32)).astype(jnp.bfloat16)
         mixed[c] = sum_
+        mixed_store(c).start()
 
         @pl.when(step == 0)
         def _():
@@ -394,18 +400,19 @@
         return carry
 
     lax.fori_loop(0, cams, time_part, 0)
-    loads[4].wait()
 
     def last_part(step, carry):
         c = camera_at(step)
         for peer in others:
             landed(returned, back_recv, c, peer)
-        x = returned[c].reshape(token_count, inner)
-        out[c] = (dot(x, time_out[...]) + mixed[c].astype(jnp.float32)).astype(jnp.bfloat16)
+        temporal_store(c).start()
         return carry
 
     lax.fori_loop(0, cams, last_part, 0)
 
+    for c in range(cams):
+        mixed_store(c).wait()
+        temporal_store(c).wait()
     for copy in edges:
         copy.wait_send()
     for peer in others:
@@ -427,7 +434,7 @@
     rows = token_count // peers
     bf16, f32 = jnp.bfloat16, jnp.float32
     vmem, smem, hbm = (
-        pl.BlockSpec(memory_space=space) for space in (pltpu.VMEM, pltpu.SMEM, pl.ANY)
+        pl.BlockSpec(memory_space=space) for space in (pltpu.VMEM, pltpu.SMEM, pltpu.HBM)
     )
     dma = pltpu.SemaphoreType.DMA
     scratch = [
@@ -435,7 +442,6 @@
         pltpu.VMEM(cross_qkv.shape[::-1], bf16),
         pltpu.VMEM(cross_out.shape, bf16),
         pltpu.VMEM(time_qkv.shape[::-1], bf16),
-        pltpu.VMEM(time_out.shape, bf16),
         pltpu.VMEM((2, token_count, width), bf16),
         pltpu.VMEM((token_count, inner), bf16),
         pltpu.VMEM((cams, token_count, inner), bf16),
@@ -456,7 +462,8 @@
         pltpu.VMEM((8, token_count), jnp.int32),
         pltpu.VMEM((peers, 8, token_count), jnp.int32),
         pltpu.VMEM((2, 8, token_count), jnp.int32),
-        dma((5,)),
+        dma((4,)),
+        dma((2 * cams,)),
         dma((2,)),
         dma((2,)),
         dma((peers,)),
@@ -472,14 +479,17 @@
         dma((cams, peers)),
         dma((cams, peers)),
     ]
-    result = pl.pallas_call(
+    temporal, mixed = pl.pallas_call(
         functools.partial(block_kernel, peers, cam_peers),
-        out_shape=jax.ShapeDtypeStruct((cams, token_count, width), bf16),
-        in_specs=[smem, smem, hbm, vmem, hbm, hbm, hbm, hbm],
-        out_specs=vmem,
+        out_shape=[
+            jax.ShapeDtypeStruct((cams, peers, rows, inner), bf16),
+            jax.ShapeDtypeStruct((cams, token_count, width), bf16),
+        ],
+        in_specs=[smem, smem, hbm, vmem, hbm, hbm, hbm],
+        out_specs=[hbm, hbm],
         scratch_shapes=scratch,
         compiler_params=pltpu.CompilerParams(
-            collective_id=0, has_side_effects=True, vmem_limit_bytes=58 * 2**20
+            collective_id=0, has_side_effects=True, vmem_limit_bytes=57 * 2**20
         ),
     )(
         counts.T,
@@ -489,9 +499,9 @@
         cross_qkv.T,
         cross_out,
         time_qkv.T,
-        time_out,
-    )
-    return result.reshape(tokens.shape)
+    )
+    result = project(temporal.reshape(cams, token_count, inner), time_out) + mixed.astype(f32)
+    return result.astype(bf16).reshape(tokens.shape)
 
 
 def passed_along(x, axis, by):

time: 61.5 us -> 62.1 us (level)
  matrix products: 0 us -> 3.65 us
  local copies, waits for them, and re-layouts: 2.37 us -> 0.01 us
  Pallas kernels: 59 us -> 58.2 us
    dot_general x0 -> x1, matrix products: none -> 3.65 us  [project(): result = jnp.dot(flat, weight, preferred_element_type=jnp.float32)]
    unnamed x1 -> x2, local copies, waits for them, and re-layouts: 2.37 us -> 0.01 us
    pallas_call x1, Pallas kernels: 59 us -> 58.2 us  [whole_block(): pl.pallas_call(functools.partial(block_kernel, peers, cam_peers), out_sha...]
where the time goes in v4:
time: 62.1 us; the launch traced here: 61.9 us
  Pallas kernels  58.2 us (94%)
  matrix products  3.65 us (6%)
    pallas_call x1, Pallas kernels, whole_block(): pl.pallas_call(functools.partial(block_kernel, peers, cam_peers), out_sha...  58.2 us
    dot_general x1, matrix products, project(): result = jnp.dot(flat, weight, preferred_element_type=jnp.float32)  3.65 us

profile of v4, /device:TPU:0, one launch (start us, length us, event | category | flops | bytes accessed | tf_op | source)
XLA Modules:
  0.0 61.9 jit_solution(17874921415127886246)
XLA Ops:
  0.0 0.0 copy-start
  0.0 58.2 %shard_map.82 = (bf16[2,8,32,576]{3,2,1,0:T(8,128)(2,1)}, bf16[2,256,1152]{2,1,0:T(8,128)(2,1)}) custom-call(s32[1,2]{1,0:T(1,128)} %bitcast.16, s32[2,2]{1,0:T(2,128)} %neighbours.1, bf16[2,256,1152]{2,1,0:T(8,128)(2,1)} %bitcast.15, bf16[2,576]{1,0:T(2,128)(2,1)} %side_keys.1, bf16[1728,1152]{1,0:T(8,128)(2,1)} %bitcast.13, ...), custom_call_target="tpu_custom_call" | custom-call | tf_op jit(solution)/shard_map/pallas_call | solution.py:482
  58.2 0.0 copy-done
  58.3 3.6 %fusion.1 = bf16[2,1,256,1152]{3,2,1,0:T(8,128)(2,1)} fusion(bf16[2,256,576]{2,1,0:T(8,128)(2,1)} %bitcast.17, bf16[2,256,1152]{2,1,0:T(8,128)(2,1)} %get-tuple-element.8, bf16[576,1152]{1,0:T(8,128)(2,1)S(1)} %copy-done), kind=kOutput, calls=%fused_computation.2 | convolution fusion | flops 681246720 | bytes 4276224 | tf_op jit(solution)/shard_map/dot_general | solution.py:514
Async XLA Ops:
  0.0 58.3 %copy-start = (bf16[576,1152]{1,0:T(8,128)(2,1)S(1)}, bf16[576,1152]{1,0:T(8,128)(2,1)}, u32[]{:S(2)}) copy-start(bf16[576,1152]{1,0:T(8,128)(2,1)} %param.15) | copy-start | bytes 3981316

commit v5 on v3

--- a/solution.py
+++ b/solution.py
@@ -71,7 +71,7 @@
     cross_out_hbm,
     time_qkv_hbm,
     time_out_hbm,
-    out,
+    out_hbm,
     tokens,
     cross_qkv,
     cross_out,
@@ -86,9 +86,12 @@
     far_values,
     normal,
     mixed,
+    out,
     leaving,
     arrived,
     early,
+    leaving_more,
+    arrived_more,
     crossed,
     late,
     incoming,
@@ -98,6 +101,7 @@
     count_in,
     count_edge,
     load_sem,
+    store_sem,
     edge_send,
     edge_recv,
     count_send,
@@ -110,6 +114,8 @@
     go_recv,
     late_send,
     late_recv,
+    more_send,
+    more_recv,
     back_send,
     back_recv,
 ):
@@ -117,6 +123,7 @@
     inner = cross_out.shape[0]
     heads = Heads(inner)
     rows = token_count // peers
+    some = rows // 2
     me = lax.axis_index("frame")
     cam = lax.axis_index("cam")
     above = lax.rem(cam + 1, cam_peers)
@@ -191,7 +198,7 @@
 
     def early_copy(peer):
         return remote(
-            tokens_hbm.at[camera_at(1), pl.ds(pl.multiple_of(peer * rows, rows), rows)],
+            tokens_hbm.at[camera_at(1), pl.ds(pl.multiple_of(peer * rows + some, some), some)],
             early.at[me],
             early_send.at[peer],
             early_recv.at[me],
@@ -243,9 +250,21 @@
     def with_side(key, side):
         return (key.astype(jnp.float32) + side).astype(jnp.bfloat16)
 
+    def out_store(c):
+        return pltpu.make_async_copy(out.at[c], out_hbm.at[c], store_sem.at[c])
+
     def go_copy(peer):
         return remote(
             leaving.at[peer], arrived.at[me], go_send.at[peer], go_recv.at[me], {"frame": peer}
+        )
+
+    def more_copy(peer):
+        return remote(
+            leaving_more.at[peer],
+            arrived_more.at[me],
+            more_send.at[peer],
+            more_recv.at[me],
+            {"frame": peer},
         )
 
     def late_copy(peer):
@@ -318,11 +337,15 @@
 
         @pl.when(step == 1)
         def _():
-            crossed[...] = result.reshape(peers, rows, inner)
+            crossed[...] = result.reshape(peers, rows, inner)[:, some:]
             for peer in others:
                 late_copy(peer).start()
+            leaving_more[...] = normalize(sum_).reshape(peers, rows, width)[:, :some]
+            for peer in others:
+                more_copy(peer).start()
             late[me] = crossed[me]
-            early[me] = tokens[c, pl.ds(pl.multiple_of(me * rows, rows), rows), :]
+            early[me] = tokens[c, pl.ds(pl.multiple_of(me * rows + some, some), some), :]
+            arrived_more[me] = leaving_more[me]
 
         return carry
 
@@ -368,9 +391,13 @@
             for peer in others:
                 landed(early, early_recv, peer)
                 landed(late, late_recv, peer)
-            again = dot(late[...].reshape(token_count, inner), cross_out[...])
-            again = again + early[...].reshape(token_count, width).astype(jnp.float32)
-            incoming[...] = normalize(again.astype(jnp.bfloat16))
+            again = dot(late[...].reshape(peers * some, inner), cross_out[...])
+            again = again + early[...].reshape(peers * some, width).astype(jnp.float32)
+            again = normalize(again.astype(jnp.bfloat16)).reshape(peers, some, width)
+            for peer in others:
+                landed(arrived_more, more_recv, peer)
+            both = jnp.concatenate([arrived_more[...], again], axis=1)
+            incoming[...] = both.reshape(token_count, width)
 
         x = incoming[...]
         query[...] = dot_t(x, time_qkv[:inner, :]).astype(jnp.bfloat16)
@@ -402,10 +429,13 @@
             landed(returned, back_recv, c, peer)
         x = returned[c].reshape(token_count, inner)
         out[c] = (dot(x, time_out[...]) + mixed[c].astype(jnp.float32)).astype(jnp.bfloat16)
+        out_store(c).start()
         return carry
 
     lax.fori_loop(0, cams, last_part, 0)
 
+    for c in range(cams):
+        out_store(c).wait()
     for copy in edges:
         copy.wait_send()
     for peer in others:
@@ -413,8 +443,35 @@
         early_copy(peer).wait_send()
         go_copy(peer).wait_send()
         late_copy(peer).wait_send()
+        more_copy(peer).wait_send()
         for c in range(cams):
             back_copy(c, peer).wait_send()
+
+
+def copy_kernel(pieces, source, target, sem):
+    size = source.shape[0] // pieces
+    copies = [
+        pltpu.make_async_copy(
+            source.at[pl.ds(i * size, size)], target.at[pl.ds(i * size, size)], sem.at[i]
+        )
+        for i in range(pieces)
+    ]
+    for copy in copies:
+        copy.start()
+    for copy in copies:
+        copy.wait()
+
+
+def copied(x, pieces):
+    flat = x.reshape(-1, x.shape[-1])
+    space = pl.BlockSpec(memory_space=pltpu.HBM)
+    return pl.pallas_call(
+        functools.partial(copy_kernel, pieces),
+        out_shape=jax.ShapeDtypeStruct(flat.shape, flat.dtype),
+        in_specs=[space],
+        out_specs=space,
+        scratch_shapes=[pltpu.SemaphoreType.DMA((pieces,))],
+    )(flat)
 
 
 def whole_block(
@@ -427,7 +484,7 @@
     rows = token_count // peers
     bf16, f32 = jnp.bfloat16, jnp.float32
     vmem, smem, hbm = (
-        pl.BlockSpec(memory_space=space) for space in (pltpu.VMEM, pltpu.SMEM, pl.ANY)
+        pl.BlockSpec(memory_space=space) for space in (pltpu.VMEM, pltpu.SMEM, pltpu.HBM)
     )
     dma = pltpu.SemaphoreType.DMA
     scratch = [
@@ -445,11 +502,14 @@
         pltpu.VMEM((token_count, inner), bf16),
         pltpu.VMEM((cams, token_count, width), bf16),
         pltpu.VMEM((cams, token_count, width), bf16),
+        pltpu.VMEM((cams, token_count, width), bf16),
         pltpu.VMEM((peers, rows, width), bf16),
         pltpu.VMEM((peers, rows, width), bf16),
-        pltpu.VMEM((peers, rows, width), bf16),
-        pltpu.VMEM((peers, rows, inner), bf16),
-        pltpu.VMEM((peers, rows, inner), bf16),
+        pltpu.VMEM((peers, rows // 2, width), bf16),
+        pltpu.VMEM((peers, rows // 2, width), bf16),
+        pltpu.VMEM((peers, rows // 2, width), bf16),
+        pltpu.VMEM((peers, rows // 2, inner), bf16),
+        pltpu.VMEM((peers, rows // 2, inner), bf16),
         pltpu.VMEM((token_count, width), bf16),
         pltpu.VMEM((cams, peers, rows, inner), bf16),
         pltpu.VMEM((cams, peers, rows, inner), bf16),
@@ -457,12 +517,15 @@
         pltpu.VMEM((peers, 8, token_count), jnp.int32),
         pltpu.VMEM((2, 8, token_count), jnp.int32),
         dma((5,)),
+        dma((cams,)),
         dma((2,)),
         dma((2,)),
         dma((peers,)),
         dma((peers,)),
         dma((2,)),
         dma((2,)),
+        dma((peers,)),
+        dma((peers,)),
         dma((peers,)),
         dma((peers,)),
         dma((peers,)),
@@ -476,7 +539,7 @@
         functools.partial(block_kernel, peers, cam_peers),
         out_shape=jax.ShapeDtypeStruct((cams, token_count, width), bf16),
         in_specs=[smem, smem, hbm, vmem, hbm, hbm, hbm, hbm],
-        out_specs=vmem,
+        out_specs=hbm,
         scratch_shapes=scratch,
         compiler_params=pltpu.CompilerParams(
             collective_id=0, has_side_effects=True, vmem_limit_bytes=58 * 2**20
@@ -491,7 +554,7 @@
         time_qkv.T,
         time_out,
     )
-    return result.reshape(tokens.shape)
+    return copied(result, 8).reshape(tokens.shape)
 
 
 def passed_along(x, axis, by):
@@ -600,7 +663,7 @@
         and frames == 1
         and lax.axis_size("cam") > 2
         and token_count == 256
-        and token_count % (16 * peers) == 0
+        and token_count % (32 * peers) == 0
     )
     chosen = whole_block if fits else plain_block
     return chosen(

time: 61.5 us -> 93.4 us (1.52)
  Pallas kernels: 59 us -> 93.2 us
  local copies, waits for them, and re-layouts: 2.37 us -> 0 us
    pallas_call x0 -> x1, Pallas kernels: none -> 36.9 us  [copied(): pl.pallas_call(functools.partial(copy_kernel, pieces), out_shape=jax.Shap...]
    pallas_call x1, Pallas kernels: 59 us -> 56.3 us  [whole_block(): pl.pallas_call(functools.partial(block_kernel, peers, cam_peers), out_sha...]
    unnamed x1 -> x0, local copies, waits for them, and re-layouts: 2.37 us -> none
where the time goes in v5:
time: 93.4 us; the launch traced here: 93.3 us
  Pallas kernels  93.2 us (100%)
    pallas_call x1, Pallas kernels, whole_block(): pl.pallas_call(functools.partial(block_kernel, peers, cam_peers), out_sha...  56.3 us
    pallas_call x1, Pallas kernels, copied(): pl.pallas_call(functools.partial(copy_kernel, pieces), out_shape=jax.Shap...  36.9 us

profile of v5, /device:TPU:0, one launch (start us, length us, event | category | flops | bytes accessed | tf_op | source)
XLA Modules:
  0.0 93.3 jit_solution(14377612916491786831)
XLA Ops:
  0.0 56.3 %shard_map.82 = bf16[2,256,1152]{2,1,0:T(8,128)(2,1)} custom-call(s32[1,2]{1,0:T(1,128)} %bitcast.12, s32[2,2]{1,0:T(2,128)} %neighbours.1, bf16[2,256,1152]{2,1,0:T(8,128)(2,1)} %bitcast.11, bf16[2,576]{1,0:T(2,128)(2,1)} %side_keys.1, bf16[1728,1152]{1,0:T(8,128)(2,1)} %bitcast.9, bf16[576,1152]{1,0:T(8,128)(2,1)} %cross_out_hbm.1, ...), custom_call_target="tpu_custom_call" | custom-call | tf_op jit(solution)/shard_map/pallas_call | solution.py:538
  56.3 36.9 %shard_map.83 = bf16[512,1152]{1,0:T(8,128)(2,1)} custom-call(bf16[512,1152]{1,0:T(8,128)(2,1)} %bitcast.8), custom_call_target="tpu_custom_call" | custom-call | tf_op jit(solution)/shard_map/pallas_call | solution.py:468
